TPU v7x, 128 devices: a whole 4x4x4 slice. The times are simulated.
128 devices in a mesh: grp: 16 (over y, z), tri: 8 (over x, core).
Axes of the slice: x: 4, y: 4, z: 4, core: 2. Of those that a mesh axis runs over, the one named last changes fastest.
Arguments:
- samples: bfloat16 [2048, 647168], P(('grp', 'tri')), may hold values from -6 to 6
- fir_taps: float32 [16, 8192], replicated, may hold values from -1.5 to 1.5
- channel_group: int32 [512], replicated, may hold values from 0 to 15, as said below
- tile_pairs: int32 [2, 136], P(None, 'tri'), may hold values from 0 to 15, as said below
Outputs:
- visibilities: bfloat16 [64, 136, 2, 128, 128], P('grp', 'tri')
Inputs may be any that keep to these rules, and one draw needn't show every extreme that they name: `channel_group`: each group is named by exactly 32 channels. `tile_pairs`: every pair of blocks with row <= column appears in exactly one slot.
All inputs are finite; a program needn't handle non-finite values.
Results may differ from a plain program's by a relative error of at most 0.0071.
Values may be sent and summed in bfloat16 or wider, within the bound.
A program may use at most 192 MiB of HBM per device.

v0:
```python
import math

import jax
import jax.numpy as jnp
from jax import lax
from jax.sharding import PartitionSpec as P

NFFT = 8192
TAPS = 16
BLOCK = 128
FIRST_CH = 1024
CH_GRP = 32
FAVG = 8
SPECTRA = 64
NBLK = 16


def dft_table(channels):
    sample_index = jnp.arange(NFFT, dtype=jnp.int32)[:, None]
    channel_index = FIRST_CH + jnp.arange(channels, dtype=jnp.int32)[None, :]
    phases = (sample_index * channel_index % NFFT).astype(jnp.float32)
    angles = phases * (2.0 * math.pi / NFFT)
    norm_scale = 1.0 / math.sqrt(NFFT)
    return jnp.concatenate(
        [jnp.cos(angles) * norm_scale, -jnp.sin(angles) * norm_scale], axis=1
    ).astype(jnp.bfloat16)


def polyphase(frames, fir_taps):
    spectra_count = frames.shape[1] - TAPS + 1
    accumulated = jnp.zeros((frames.shape[0], spectra_count, NFFT), jnp.float32)
    for tap_index in range(TAPS):
        accumulated = (
            accumulated
            + frames[:, tap_index : tap_index + spectra_count].astype(jnp.float32)
            * fir_taps[tap_index]
        )
    return accumulated.astype(jnp.bfloat16)


def tile_products(channel_data, tile_rows, tile_cols):
    turned = jnp.concatenate([channel_data[..., SPECTRA:], -channel_data[..., :SPECTRA]], axis=3)
    row_blocks = jnp.concatenate(
        [jnp.take(channel_data, tile_rows, axis=1), jnp.take(turned, tile_rows, axis=1)], axis=2
    )
    col_blocks = jnp.take(channel_data, tile_cols, axis=1)
    products = jnp.einsum(
        "qtis,qtjs->tij", row_blocks, col_blocks, preferred_element_type=jnp.float32
    )
    return (products * (1.0 / (SPECTRA * FAVG))).reshape(tile_rows.shape[0], 2, BLOCK, BLOCK)


def shards(samples, fir_taps, channel_group, tile_pairs):
    dish_dev = samples.shape[0]
    channels = channel_group.shape[0]
    groups = lax.axis_size("grp")
    tri_size = lax.axis_size("tri")
    frames = samples.reshape(dish_dev, SPECTRA + TAPS - 1, NFFT)
    filtered = polyphase(frames, fir_taps)
    flat_spectra = jnp.dot(
        filtered.reshape(-1, NFFT), dft_table(channels), preferred_element_type=jnp.float32
    )
    spectra = flat_spectra.astype(jnp.bfloat16).reshape(dish_dev, SPECTRA, 2, channels)
    same_group = channel_group[:, None] == channel_group[None, :]
    earlier = jnp.arange(channels)[None, :] < jnp.arange(channels)[:, None]
    channel_rank = jnp.sum(same_group & earlier, axis=1)
    slot_ids = jnp.arange(CH_GRP, dtype=jnp.int32)[:, None, None]
    group_ids = jnp.arange(groups, dtype=jnp.int32)[None, :, None]
    selector = (
        (channel_group[None, None, :] == group_ids) & (channel_rank[None, None, :] == slot_ids)
    ).astype(jnp.bfloat16)
    outgoing = jnp.einsum(
        "qgc,dsrc->qgdrs", selector, spectra, preferred_element_type=jnp.float32
    ).astype(jnp.bfloat16)
    outgoing = outgoing.reshape(CH_GRP, groups, 1, dish_dev, 2 * SPECTRA)
    copies = jnp.broadcast_to(outgoing, (CH_GRP, groups, tri_size, dish_dev, 2 * SPECTRA))
    copies = copies.reshape(CH_GRP, groups * tri_size, dish_dev, 2 * SPECTRA)
    arrived = lax.all_to_all(copies, ("grp", "tri"), split_axis=1, concat_axis=1, tiled=True)
    voltages = arrived.reshape(CH_GRP // FAVG, FAVG, NBLK, BLOCK, 2 * SPECTRA)
    tile_rows = tile_pairs[0]
    tile_cols = tile_pairs[1]

    def correlate(channel_data):
        return tile_products(channel_data, tile_rows, tile_cols).astype(jnp.bfloat16)

    return lax.map(correlate, voltages)


def solution(mesh):
    in_specs = (P(("grp", "tri"), None), P(), P(), P(None, "tri"))
    out_specs = P("grp", "tri", None, None, None)
    return jax.shard_map(shards, mesh=mesh, in_specs=in_specs, out_specs=out_specs, check_vma=False)
```

profile of v0, /device:TPU:68, one launch (start us, length us, event | category | flops | bytes accessed | tf_op | source)
XLA Modules:
  0.0 726.9 jit_solution(5007691185786824057)
XLA Ops:
  1.7 3.4 fusion.36
  5.1 26.9 %reshape.103 = bf16[16,79,8192]{2,1,0:T(8,128)(2,1)} reshape(bf16[16,647168]{1,0:T(8,128)(2,1)} %param.8) | data formatting | bytes 41418752 | tf_op jit(solution)/shard_map/reshape | solution.py:58
  32.0 69.6 %multiply_convert_fusion.1 = (bf16[8192,512]{1,0:T(8,128)(2,1)}, bf16[8192,512]{1,0:T(8,128)(2,1)}) fusion(s32[512]{0:T(512)S(1)} %iota_add_fusion), kind=kLoop, calls=%fused_computation.39 | loop fusion | flops 79691776 | bytes 16779264 | tf_op jit(solution)/shard_map/convert
  101.5 131.5 %add_convert_fusion = bf16[16,64,8192]{2,1,0:T(8,128)(2,1)} fusion(bf16[16,79,8192]{2,1,0:T(8,128)(2,1)} %reshape.103, f32[8192]{0:T(1024)S(1)} %bitcast.80, f32[8192]{0:T(1024)S(1)} %bitcast.81, f32[8192]{0:T(1024)S(1)} %bitcast.67, f32[8192]{0:T(1024)S(1)} %bitcast.68, f32[8192]{0:T(1024)S(1)} %bitcast.69, f32[8192]{0:T(1024)S(1)} %bitcast.70, ...), kind=kLoop, calls=%fused_computation.27 | loop fusion | flops 402653184 | bytes 285736960 | tf_op jit(solution)/shard_map/convert_element_type | solution.py:38
  233.1 23.2 %fusion.26 = bf16[1024,1024]{1,0:T(8,128)(2,1)} fusion(bf16[1024,8192]{1,0:T(8,128)(2,1)} %bitcast.64, bf16[8192,512]{1,0:T(8,128)(2,1)} %get-tuple-element.69, bf16[8192,512]{1,0:T(8,128)(2,1)} %get-tuple-element.68), kind=kOutput, calls=%fused_computation.45 | convolution fusion | flops 17214472192 | bytes 35651584 | tf_op jit(solution)/shard_map/dot_general | solution.py:60
  256.3 3.3 reshape.105
  259.6 2.8 convert_bitcast_fusion
  262.4 6.3 copy.24
  268.7 6.8 reshape.144
  275.5 6.2 broadcast_in_dim.15
  281.7 10.9 %all-to-all-start = ((bf16[32,128,16,128]{3,2,0,1:T(8,128)(2,1)}), bf16[32,128,16,128]{3,2,0,1:T(8,128)(2,1)}, u32[]{:S(2)}, u32[]{:S(2)}) async-start(bf16[32,128,16,128]{3,2,0,1:T(8,128)(2,1)} %bitcast.62), calls=%async_computation | async-start | bytes 33554432 | tf_op jit(solution)/shard_map/all_to_all | solution.py:78
  292.6 241.5 %all-to-all-done = bf16[32,128,16,128]{3,2,0,1:T(8,128)(2,1)} async-done(((bf16[32,128,16,128]{3,2,0,1:T(8,128)(2,1)}), bf16[32,128,16,128]{3,2,0,1:T(8,128)(2,1)}, u32[]{:S(2)}, u32[]{:S(2)}) %all-to-all-start) | async-done | bytes 16777248 | tf_op jit(solution)/shard_map/all_to_all | solution.py:78
  534.1 14.5 %copy.18 = bf16[32,128,16,128]{3,2,1,0:T(8,128)(2,1)} copy(bf16[32,128,16,128]{3,2,0,1:T(8,128)(2,1)} %all-to-all-done) | data formatting | bytes 33554432 | tf_op jit(solution)/shard_map/all_to_all | solution.py:78
  548.7 178.0 %while.10 = (s32[]{:T(128)}, bf16[4,17,2,128,128]{4,3,2,1,0:T(8,128)(2,1)}, bf16[4,8,16,128,128]{4,3,2,1,0:T(8,128)(2,1)}, s32[17]{0:T(128)S(1)}, s32[17]{0:T(128)S(1)}, /*index=5*/s32[]{:T(128)}) while((s32[]{:T(128)}, bf16[4,17,2,128,128]{4,3,2,1,0:T(8,128)(2,1)}, bf16[4,8,16,128,128]{4,3,2,1,0:T(8,128)(2,1)}, s32[17]{0:T(128)S(1)}, ...), condition=%wide.region_2.4_spmd, body=%wide.region_1.3_spmd.sunk | while | flops 1175914752 | bytes 103228824 | solution.py:86
  548.7 2.5 dynamic-slice_bitcast_fusion.2
  551.2 1.9 copy-done
  553.1 1.7 fusion.44
  554.8 3.8 pad_maximum_fusion.2
  558.6 6.0 gather_fusion.2
  564.6 6.1 gather_fusion.1
  570.7 7.9 %select_bitcast_fusion.3 = (bf16[8,17,128,128]{3,2,0,1:T(8,128)(2,1)}, bf16[8,17,128,128]{3,2,0,1:T(8,128)(2,1)}) fusion(bf16[17,8,128,128]{3,2,1,0:T(8,128)(2,1)} %gather_fusion.1, pred[17]{0:T(512)(128)(4,1)S(1)} %get-tuple-element.114, bf16[17,8,128,128]{3,2,1,0:T(8,128)(2,1)} %gather_fusion.2), kind=kLoop, calls=%fused_computation.10.clone.1 | loop fusion | flops 4456448 | bytes 17825808 | tf_op jit(solution)/shard_map/while/body/eval_jaxpr/jit(_take)/select_n | solution.py:44
  578.6 6.1 gather_fusion
  584.7 7.4 %fusion.45 = bf16[17,256,128]{2,1,0:T(8,128)(2,1)S(1)} fusion(bf16[17,8,128,128]{3,2,1,0:T(8,128)(2,1)} %gather_fusion, pred[17]{0:T(512)(128)(4,1)S(1)} %get-tuple-element.112, bf16[8,17,128,128]{3,2,0,1:T(8,128)(2,1)} %get-tuple-element.117, bf16[8,17,128,128]{3,2,0,1:T(8,128)(2,1)} %get-tuple-element.118), kind=kOutput, calls=%fused_computation.16.clone.1 | convolution fusion | flops 1162018816 | bytes 14483473 | tf_op jit(solution)/shard_map/while/body/eval_jaxpr/qtis,qtjs->tij/dot_general | solution.py:47
  593.2 2.5 dynamic-slice_bitcast_fusion.2
  595.7 1.9 copy-done
  597.6 1.7 fusion.44
  599.3 3.8 pad_maximum_fusion.2
  603.1 6.0 gather_fusion.2
  609.1 6.1 gather_fusion.1
  615.2 7.9 %select_bitcast_fusion.3 = (bf16[8,17,128,128]{3,2,0,1:T(8,128)(2,1)}, bf16[8,17,128,128]{3,2,0,1:T(8,128)(2,1)}) fusion(bf16[17,8,128,128]{3,2,1,0:T(8,128)(2,1)} %gather_fusion.1, pred[17]{0:T(512)(128)(4,1)S(1)} %get-tuple-element.114, bf16[17,8,128,128]{3,2,1,0:T(8,128)(2,1)} %gather_fusion.2), kind=kLoop, calls=%fused_computation.10.clone.1 | loop fusion | flops 4456448 | bytes 17825808 | tf_op jit(solution)/shard_map/while/body/eval_jaxpr/jit(_take)/select_n | solution.py:44
  623.1 6.1 gather_fusion
  629.2 7.4 %fusion.45 = bf16[17,256,128]{2,1,0:T(8,128)(2,1)S(1)} fusion(bf16[17,8,128,128]{3,2,1,0:T(8,128)(2,1)} %gather_fusion, pred[17]{0:T(512)(128)(4,1)S(1)} %get-tuple-element.112, bf16[8,17,128,128]{3,2,0,1:T(8,128)(2,1)} %get-tuple-element.117, bf16[8,17,128,128]{3,2,0,1:T(8,128)(2,1)} %get-tuple-element.118), kind=kOutput, calls=%fused_computation.16.clone.1 | convolution fusion | flops 1162018816 | bytes 14483473 | tf_op jit(solution)/shard_map/while/body/eval_jaxpr/qtis,qtjs->tij/dot_general | solution.py:47
  637.7 2.5 dynamic-slice_bitcast_fusion.2
  640.2 1.9 copy-done
  643.8 3.8 pad_maximum_fusion.2
  647.6 6.0 gather_fusion.2
  653.6 6.1 gather_fusion.1
  659.7 7.9 %select_bitcast_fusion.3 = (bf16[8,17,128,128]{3,2,0,1:T(8,128)(2,1)}, bf16[8,17,128,128]{3,2,0,1:T(8,128)(2,1)}) fusion(bf16[17,8,128,128]{3,2,1,0:T(8,128)(2,1)} %gather_fusion.1, pred[17]{0:T(512)(128)(4,1)S(1)} %get-tuple-element.114, bf16[17,8,128,128]{3,2,1,0:T(8,128)(2,1)} %gather_fusion.2), kind=kLoop, calls=%fused_computation.10.clone.1 | loop fusion | flops 4456448 | bytes 17825808 | tf_op jit(solution)/shard_map/while/body/eval_jaxpr/jit(_take)/select_n | solution.py:44
  667.6 6.1 gather_fusion
  673.7 7.4 %fusion.45 = bf16[17,256,128]{2,1,0:T(8,128)(2,1)S(1)} fusion(bf16[17,8,128,128]{3,2,1,0:T(8,128)(2,1)} %gather_fusion, pred[17]{0:T(512)(128)(4,1)S(1)} %get-tuple-element.112, bf16[8,17,128,128]{3,2,0,1:T(8,128)(2,1)} %get-tuple-element.117, bf16[8,17,128,128]{3,2,0,1:T(8,128)(2,1)} %get-tuple-element.118), kind=kOutput, calls=%fused_computation.16.clone.1 | convolution fusion | flops 1162018816 | bytes 14483473 | tf_op jit(solution)/shard_map/while/body/eval_jaxpr/qtis,qtjs->tij/dot_general | solution.py:47
  682.2 2.5 dynamic-slice_bitcast_fusion.2
  684.7 1.9 copy-done
  688.3 3.8 pad_maximum_fusion.2
  692.1 6.0 gather_fusion.2
  698.1 6.1 gather_fusion.1
  704.2 7.9 %select_bitcast_fusion.3 = (bf16[8,17,128,128]{3,2,0,1:T(8,128)(2,1)}, bf16[8,17,128,128]{3,2,0,1:T(8,128)(2,1)}) fusion(bf16[17,8,128,128]{3,2,1,0:T(8,128)(2,1)} %gather_fusion.1, pred[17]{0:T(512)(128)(4,1)S(1)} %get-tuple-element.114, bf16[17,8,128,128]{3,2,1,0:T(8,128)(2,1)} %gather_fusion.2), kind=kLoop, calls=%fused_computation.10.clone.1 | loop fusion | flops 4456448 | bytes 17825808 | tf_op jit(solution)/shard_map/while/body/eval_jaxpr/jit(_take)/select_n | solution.py:44
  712.1 6.1 gather_fusion
  718.2 7.4 %fusion.45 = bf16[17,256,128]{2,1,0:T(8,128)(2,1)S(1)} fusion(bf16[17,8,128,128]{3,2,1,0:T(8,128)(2,1)} %gather_fusion, pred[17]{0:T(512)(128)(4,1)S(1)} %get-tuple-element.112, bf16[8,17,128,128]{3,2,0,1:T(8,128)(2,1)} %get-tuple-element.117, bf16[8,17,128,128]{3,2,0,1:T(8,128)(2,1)} %get-tuple-element.118), kind=kOutput, calls=%fused_computation.16.clone.1 | convolution fusion | flops 1162018816 | bytes 14483473 | tf_op jit(solution)/shard_map/while/body/eval_jaxpr/qtis,qtjs->tij/dot_general | solution.py:47
  (34 shorter events, 9.5 us)
Async XLA Ops:
  281.7 10.9 %copy-start.1 = (s32[2,17]{1,0:T(2,128)S(1)}, s32[2,17]{1,0:T(2,128)}, u32[]{:S(2)}) copy-start(s32[2,17]{1,0:T(2,128)} %param.11) | copy-start | bytes 412
  281.7 252.4 %all-to-all-start = ((bf16[32,128,16,128]{3,2,0,1:T(8,128)(2,1)}), bf16[32,128,16,128]{3,2,0,1:T(8,128)(2,1)}, u32[]{:S(2)}, u32[]{:S(2)}) async-start(bf16[32,128,16,128]{3,2,0,1:T(8,128)(2,1)} %bitcast.62), calls=%async_computation | async-start | bytes 33554432 | tf_op jit(solution)/shard_map/all_to_all | solution.py:78
  551.2 1.9 copy-start
  595.7 1.9 copy-start
  640.2 1.9 copy-start
  684.7 1.9 copy-start
where the time goes:
time: 735 us; the launch traced here: 727 us
  other arithmetic  256 us (35%)
  waiting for transfers between devices  241 us (33%)
  local copies, waits for them, and re-layouts  162 us (22%)
  matrix products  55.7 us (8%)
  starting transfers between devices  10.9 us (1%)
    all_to_all x1, waiting for transfers between devices, shards(): lax.all_to_all(copies, ('grp', 'tri'), split_axis=1, concat_axis=1, tiled...  241 us
    convert_element_type x1, other arithmetic, polyphase(): return accumulated.astype(jnp.bfloat16)  132 us
    another operation x1, other arithmetic  69.6 us
    select_n x4, other arithmetic, tile_products(): jnp.take(channel_data, tile_rows, axis=1)  31.6 us
    dot_general x4, matrix products, tile_products(): jnp.einsum('qtis,qtjs->tij', row_blocks, col_blocks, preferred_element_ty...  29.7 us
    reshape x1, local copies, waits for them, and re-layouts, shards(): frames = samples.reshape(dish_dev, SPECTRA + TAPS - 1, NFFT)  26.9 us
    gather x4, local copies, waits for them, and re-layouts, tile_products(): jnp.take(channel_data, tile_rows, axis=1)  24.4 us
    gather x4, local copies, waits for them, and re-layouts, tile_products(): col_blocks = jnp.take(channel_data, tile_cols, axis=1)  24.3 us
  transfers between devices with their start and end apart: 1, of which 1 were waited for; matrix products, arithmetic and copies ran while one was open for 0% of the time, Pallas kernels for 0%

commit v1 on v0

v1 whole, which is shorter than its diff:
```python
import math

import jax
import jax.numpy as jnp
import numpy as np
from jax import lax
from jax.experimental import pallas as pl
from jax.experimental.pallas import tpu as pltpu
from jax.sharding import PartitionSpec as P

NFFT = 8192
TAPS = 16
BLOCK = 128
FIRST_CH = 1024
CHANNELS = 512
CH_GRP = 32
FAVG = 8
SPECTRA = 64
NBLK = 16
DISH = 16
GROUPS = 16
TRI = 8
ROWS = CH_GRP // FAVG
FSTEP = 8
CHUNKS = SPECTRA // FSTEP
MROWS = FSTEP * DISH
RADIX = 8
SUB = NFFT // RADIX
RESIDUES = (0, 4, 1, 7, 2, 6, 3, 5)
MESH = pl.DeviceIdType.MESH


def twiddle_tables():
    n = np.arange(SUB, dtype=np.int64)[:, None]
    k2 = np.arange(CHANNELS // RADIX, dtype=np.int64)[None, :]
    scale = 1.0 / math.sqrt(NFFT)
    tables = np.zeros((4, 2 * SUB, 256), np.float64)
    for pair in range(4):
        for which in range(2):
            residue = RESIDUES[2 * pair + which]
            channel = FIRST_CH + RADIX * k2 + residue
            angle = ((n * channel) % NFFT) * (2.0 * math.pi / NFFT)
            cos, sin = np.cos(angle) * scale, np.sin(angle) * scale
            lo = which * 128
            if pair == 0:
                rows = slice(which * SUB, (which + 1) * SUB)
                tables[pair, rows, lo : lo + 64] = cos
                tables[pair, rows, lo + 64 : lo + 128] = -sin
            else:
                sign = 1.0 if which == 0 else -1.0
                tables[pair, :SUB, lo : lo + 64] = cos
                tables[pair, SUB:, lo : lo + 64] = -sign * sin
                tables[pair, :SUB, lo + 64 : lo + 128] = -sin
                tables[pair, SUB:, lo + 64 : lo + 128] = -sign * cos
    return tables.astype(jnp.bfloat16)


def al(x):
    return pl.multiple_of(x, 128)


def channelize_kernel(
    samples, fir, tables, group_row, group_col, volts,
    xs, wt, perm, fbuf, planes, spec, send,
    x_sem, w_sem, own_sem, a2a_s, a2a_r, dir_s, dir_r, fwd_s, fwd_r, sib_s, sib_r,
):
    grp, tri = lax.axis_index("grp"), lax.axis_index("tri")
    gy, gz = grp // 4, lax.rem(grp, 4)
    cx, core = tri // 2, lax.rem(tri, 2)

    def group_at(dy, dz):
        return lax.rem(gy + dy, 4) * 4 + lax.rem(gz + dz, 4)

    def tri_at(dx):
        return lax.rem(cx + dx, 4) * 2 + core

    partners = [group_at(dy, dz) for dy in range(4) for dz in range(4) if (dy, dz) != (0, 0)]
    right, left, across = tri_at(1), tri_at(3), tri_at(2)
    sibling = cx * 2 + (1 - core)

    def frames_copy(i, count):
        cols = pl.ds(al(i * (FSTEP * NFFT)), count * NFFT)
        return pltpu.make_async_copy(samples.at[:, cols], xs.at[:, cols], x_sem.at[i])

    for i in range(3):
        frames_copy(i, FSTEP).start()
    table_copy = pltpu.make_async_copy(tables, wt, w_sem)
    table_copy.start()

    barrier = pltpu.get_barrier_semaphore()
    for p in partners:
        pl.semaphore_signal(barrier, inc=1, device_id=(p, tri), device_id_type=MESH)
    for t in (right, left, sibling):
        pl.semaphore_signal(barrier, inc=1, device_id=(grp, t), device_id_type=MESH)

    def number(shape, axis):
        i = lax.broadcasted_iota(jnp.int32, shape, axis)
        slot, k2 = i >> 6, i & 63
        residue = jnp.zeros_like(i)
        for s, r in enumerate(RESIDUES):
            residue = jnp.where(slot == s, r, residue)
        return k2 * RADIX + residue

    for piece in range(8):
        rows = pl.ds(piece * 64, 64)
        gcol = group_col[rows, :]
        shape = (64, CHANNELS)
        c_col = lax.broadcasted_iota(jnp.int32, shape, 0) * RADIX + RESIDUES[piece]
        hit = (gcol == group_row[...]) & (number(shape, 1) < c_col)
        rank = jnp.sum(hit.astype(jnp.int32), axis=1, keepdims=True)
        dst = (gcol >> 1) * 128 + (gcol & 1) * 32 + (rank >> 3) * 8 + (rank & 7)
        lane = lax.broadcasted_iota(jnp.int32, (64, 1024), 1)
        for part in range(2):
            one = (lane == dst + part * 64).astype(jnp.float32).astype(jnp.bfloat16)
            perm[pl.ds(piece * 128 + part * 64, 64), :] = one

    pl.semaphore_wait(barrier, len(partners) + 3)
    table_copy.wait()

    def a2a_copy(j, i):
        p = partners[i]
        return pltpu.make_async_remote_copy(
            src_ref=send.at[j, p], dst_ref=volts.at[j, tri, grp],
            send_sem=a2a_s.at[j], recv_sem=a2a_r.at[j],
            device_id=(p, tri), device_id_type=MESH)

    def own_copy(j):
        return pltpu.make_async_copy(send.at[j, grp], volts.at[j, tri, grp], own_sem.at[j])

    def part_copy(j, t, half, to, ssem, rsem):
        ref = volts.at[j, t] if half is None else volts.at[j, t, pl.ds(half * 8, 8)]
        return pltpu.make_async_remote_copy(
            src_ref=ref, dst_ref=ref, send_sem=ssem, recv_sem=rsem,
            device_id=(grp, to), device_id_type=MESH)

    def direct(j, way):
        return part_copy(j, tri, None, (right, left)[way], dir_s.at[way, j], dir_r.at[way, j])

    def forward(j, way):
        return part_copy(j, (left, right)[way], way, (right, left)[way], fwd_s.at[way, j], fwd_r.at[way, j])

    def share(j, which):
        return part_copy(j, (tri, left, right, across)[which], None, sibling, sib_s.at[which, j], sib_r.at[which, j])

    def stage_direct(j):
        own_copy(j).wait()
        some = volts.at[j, tri, pl.ds(0, GROUPS - 1)]
        pltpu.make_async_copy(some, some, a2a_r.at[j]).wait()
        for way in range(2):
            direct(j, way).start()
        share(j, 0).start()

    def stage_forward(j):
        for way in range(2):
            direct(j, way).wait_recv()
            forward(j, way).start()
        share(j, 1).start()
        share(j, 2).start()

    def stage_across(j):
        for way in range(2):
            forward(j, way).wait_recv()
        share(j, 3).start()

    half_root = math.sqrt(0.5)
    lane = lax.broadcasted_iota(jnp.int32, (DISH, 128), 1)

    def filter_tile(j, i):
        for n1 in range(RADIX):
            off = n1 * SUB + i * 128
            coef = [fir[pl.ds(t, 1), pl.ds(al(off), 128)] for t in range(TAPS)]
            acc = [None] * FSTEP
            for fr in range(FSTEP + TAPS - 1):
                x = xs[:, pl.ds(al((j * FSTEP + fr) * NFFT + off), 128)].astype(jnp.float32)
                for f in range(max(0, fr - TAPS + 1), min(FSTEP - 1, fr) + 1):
                    term = x * coef[fr - f]
                    acc[f] = term if acc[f] is None else acc[f] + term
                    if fr - f == TAPS - 1:
                        fbuf[n1, pl.ds(f * DISH, DISH), :] = acc[f]
        for f in range(FSTEP):
            rows = pl.ds(f * DISH, DISH)
            v = [fbuf[n1, rows, :] for n1 in range(RADIX)]
            a = [v[k] + v[k + 4] for k in range(4)]
            b = [v[k] - v[k + 4] for k in range(4)]
            even, odd = a[0] + a[2], a[1] + a[3]
            diff = (b[1] - b[3]) * half_root
            total = (b[1] + b[3]) * half_root
            out = (even + odd, even - odd, b[0] + diff, b[2] + total,
                   a[0] - a[2], a[1] - a[3], b[0] - diff, total - b[2])
            for k in range(RADIX):
                planes[rows, pl.ds(al(k * SUB + i * 128), 128)] = out[k].astype(jnp.bfloat16)

    def transform(j):
        for p in range(4):
            spec[:, p * 256 : (p + 1) * 256] = jnp.dot(
                planes[:, p * 2048 : (p + 1) * 2048], wt[p], preferred_element_type=jnp.float32
            ).astype(jnp.bfloat16)
        for blk in range(8):
            got = jnp.dot(spec[...], perm[:, blk * 128 : (blk + 1) * 128], preferred_element_type=jnp.float32)
            t = [got[f * DISH : (f + 1) * DISH] for f in range(FSTEP)]
            for bit in range(3):
                step = 1 << bit
                odd = (lane >> (3 + bit)) & 1 == 1
                new = list(t)
                for k in range(FSTEP):
                    if not k & step:
                        up = pltpu.roll(t[k + step], 8 * step, 1)
                        down = pltpu.roll(t[k], 128 - 8 * step, 1)
                        new[k] = jnp.where(odd, up, t[k])
                        new[k + step] = jnp.where(odd, t[k + step], down)
                t = new
            for k in range(FSTEP):
                send[j, blk * 2 + k // 4, k % 4] = t[k].astype(jnp.bfloat16)

    def step(s, carry):
        @pl.when(s < CHUNKS)
        def _():
            @pl.when(s + 3 < CHUNKS + 1)
            def _():
                frames_copy(s + 3, FSTEP).start()

            @pl.when(s + 3 == CHUNKS + 1)
            def _():
                frames_copy(CHUNKS + 1, FSTEP - 1).start()

            @pl.when(s == 0)
            def _():
                frames_copy(0, FSTEP).wait()
                frames_copy(1, FSTEP).wait()

            @pl.when(s + 2 < CHUNKS + 1)
            def _():
                frames_copy(s + 2, FSTEP).wait()

            @pl.when(s + 2 == CHUNKS + 1)
            def _():
                frames_copy(CHUNKS + 1, FSTEP - 1).wait()

            def tile(i, c):
                filter_tile(s, i)
                return c

            lax.fori_loop(0, SUB // 128, tile, 0)
            transform(s)
            for i in range(GROUPS - 1):
                a2a_copy(s, i).start()
            own_copy(s).start()

        @pl.when((s >= 1) & (s <= CHUNKS))
        def _():
            stage_direct(s - 1)

        @pl.when((s >= 2) & (s <= CHUNKS + 1))
        def _():
            stage_forward(s - 2)

        @pl.when(s >= 3)
        def _():
            stage_across(s - 3)

        return carry

    lax.fori_loop(0, CHUNKS + 3, step, 0)

    def finish(j, carry):
        some = send.at[j, pl.ds(0, GROUPS - 1)]
        pltpu.make_async_copy(some, some, a2a_s.at[j]).wait()
        for way in range(2):
            direct(j, way).wait_send()
            forward(j, way).wait_send()
        for which in range(4):
            share(j, which).wait()
        return carry

    lax.fori_loop(0, CHUNKS, finish, 0)


def channelize(samples, fir_taps, tables, group_row, group_col):
    dma = pltpu.SemaphoreType.DMA
    any_spec = pl.BlockSpec(memory_space=pl.ANY)
    vmem = pl.BlockSpec(memory_space=pltpu.VMEM)
    return pl.pallas_call(
        channelize_kernel,
        out_shape=jax.ShapeDtypeStruct((CHUNKS, TRI, NBLK, ROWS, DISH, 128), jnp.bfloat16),
        in_specs=[any_spec, vmem, any_spec, vmem, vmem],
        out_specs=any_spec,
        scratch_shapes=[
            pltpu.VMEM(samples.shape, jnp.bfloat16),
            pltpu.VMEM(tables.shape, jnp.bfloat16),
            pltpu.VMEM((1024, 1024), jnp.bfloat16),
            pltpu.VMEM((RADIX, MROWS, 128), jnp.float32),
            pltpu.VMEM((MROWS, NFFT), jnp.bfloat16),
            pltpu.VMEM((MROWS, 1024), jnp.bfloat16),
            pltpu.VMEM((CHUNKS, GROUPS, ROWS, DISH, 128), jnp.bfloat16),
            dma((CHUNKS + 2,)), dma, dma((CHUNKS,)), dma((CHUNKS,)), dma((CHUNKS,)),
            dma((2, CHUNKS)), dma((2, CHUNKS)), dma((2, CHUNKS)), dma((2, CHUNKS)),
            dma((4, CHUNKS)), dma((4, CHUNKS)),
        ],
        compiler_params=pltpu.CompilerParams(
            collective_id=0, has_side_effects=True, vmem_limit_bytes=58 << 20),
        name="channelize",
    )(samples, fir_taps, tables, group_row, group_col)


def correlate_kernel(pairs, volts, out, rows, turned):
    lane = lax.broadcasted_iota(jnp.int32, (BLOCK, 128), 1)
    for j in range(CHUNKS):
        cols = pl.ds(j * 128, 128)

        def arrange(b, c):
            v = volts[j, :, b, 0].reshape(BLOCK, 128)
            rows[b, :, cols] = v
            v = v.astype(jnp.float32)
            v = jnp.where(lane < 64, -1.0, 1.0) * pltpu.roll(v, 64, 1)
            turned[b, :, cols] = v.astype(jnp.bfloat16)
            return c

        lax.fori_loop(0, NBLK, arrange, 0)

    def tile(s, c):
        a, b = pairs[0, s], pairs[1, s]
        dims = (((1,), (1,)), ((), ()))
        for part, ref in enumerate((rows, turned)):
            got = lax.dot_general(rows[a], ref[b], dims, preferred_element_type=jnp.float32)
            out[0, s, part] = (got * (1.0 / (SPECTRA * FAVG))).astype(jnp.bfloat16)
        return c

    lax.fori_loop(0, out.shape[1], tile, 0)


def correlate(tile_pairs, volts):
    slots = tile_pairs.shape[1]
    return pl.pallas_call(
        correlate_kernel,
        grid_spec=pltpu.PrefetchScalarGridSpec(
            num_scalar_prefetch=1,
            grid=(ROWS,),
            in_specs=[pl.BlockSpec((CHUNKS, TRI, NBLK, 1, DISH, 128), lambda o, _: (0, 0, 0, o, 0, 0))],
            out_specs=pl.BlockSpec((1, slots, 2, BLOCK, BLOCK), lambda o, _: (o, 0, 0, 0, 0)),
            scratch_shapes=[
                pltpu.VMEM((NBLK, BLOCK, CHUNKS * 128), jnp.bfloat16),
                pltpu.VMEM((NBLK, BLOCK, CHUNKS * 128), jnp.bfloat16),
            ],
        ),
        out_shape=jax.ShapeDtypeStruct((ROWS, slots, 2, BLOCK, BLOCK), jnp.bfloat16),
        compiler_params=pltpu.CompilerParams(vmem_limit_bytes=58 << 20),
        name="correlate",
    )(tile_pairs, volts)


def shards(samples, fir_taps, channel_group, tile_pairs):
    order = np.concatenate([np.arange(r, CHANNELS, RADIX) for r in RESIDUES])
    by_residue = channel_group[order]
    volts = channelize(
        samples, fir_taps, jnp.asarray(twiddle_tables()), by_residue[None, :], by_residue[:, None]
    )
    return correlate(tile_pairs, volts)


def solution(mesh):
    in_specs = (P(("grp", "tri"), None), P(), P(), P(None, "tri"))
    out_specs = P("grp", "tri", None, None, None)
    return jax.shard_map(shards, mesh=mesh, in_specs=in_specs, out_specs=out_specs, check_vma=False)
```

time: 735 us -> 175 us (0.24)
  the two profiles are of different devices: /device:TPU:68 before, /device:TPU:1 now
where the time goes in v1:
time: 175 us
  Pallas kernels  170 us (97%)
  local copies, waits for them, and re-layouts  4.35 us (2%)
    pallas_call x1, Pallas kernels, channelize(): pl.pallas_call(channelize_kernel, out_shape=jax.ShapeDtypeStruct((CHUNKS,...  101 us
    pallas_call x1, Pallas kernels, correlate(): pl.pallas_call(correlate_kernel, grid_spec=pltpu.PrefetchScalarGridSpec(n...  68.7 us

profile of v1, /device:TPU:1, one launch (start us, length us, event | category | flops | bytes accessed | tf_op | source)
XLA Modules:
  0.0 174.7 jit_solution(8512244901536017995)
XLA Ops:
  0.0 0.0 copy-start
  0.0 0.7 pad_clamp_fusion
  0.7 0.0 copy-done
  0.7 3.5 %gather_fusion = s32[512]{0:T(512)S(1)} fusion(s32[512]{0:T(512)S(1)} %copy-done, s32[1024]{0:T(1024)S(1)} %pad_clamp_fusion), kind=kCustom, calls=%fused_computation | custom fusion | bytes 6144 | tf_op jit(solution)/shard_map/gather | solution.py:353
  4.2 0.0 copy-start.1
  4.2 0.9 copy.8.group_col
  5.1 0.0 copy-done.1
  5.1 100.9 %channelize.1.volts = bf16[8,8,16,4,16,128]{5,4,3,2,1,0:T(8,128)(2,1)} custom-call(bf16[16,647168]{1,0:T(8,128)(2,1)} %samples.1, f32[16,8192]{1,0:T(8,128)} %fir.1, bf16[4,2048,256]{2,1,0:T(8,128)(2,1)} %constant.10.clone.tables, s32[1,512]{1,0:T(1,128)} %bitcast.3, s32[512,1]{1,0:T(8,128)} %copy.8.group_col), custom_call_target="tpu_custom_call" | custom-call | tf_op jit(solution)/shard_map/channelize/pallas_call | solution.py:282
  106.0 68.7 %correlate.1 = bf16[4,17,2,128,128]{4,3,2,1,0:T(8,128)(2,1)} custom-call(s32[2,17]{1,0:T(2,128)} %pairs.1, bf16[8,8,16,4,16,128]{5,4,3,2,1,0:T(8,128)(2,1)} %channelize.1.volts), custom_call_target="tpu_custom_call" | custom-call | tf_op jit(solution)/shard_map/correlate/pallas_call | solution.py:333
Async XLA Ops:
  0.0 0.7 copy-start
  4.2 0.9 copy-start.1

commit v2 on v1

v2 whole, which is shorter than its diff:
```python
import math

import jax
import jax.numpy as jnp
import numpy as np
from jax import lax
from jax.experimental import pallas as pl
from jax.experimental.pallas import tpu as pltpu
from jax.sharding import PartitionSpec as P

NFFT = 8192
TAPS = 16
BLOCK = 128
FIRST_CH = 1024
CHANNELS = 512
CH_GRP = 32
FAVG = 8
SPECTRA = 64
NBLK = 16
DISH = 16
GROUPS = 16
TRI = 8
ROWS = CH_GRP // FAVG
FSTEP = 8
CHUNKS = SPECTRA // FSTEP
MROWS = FSTEP * DISH
RING = 4
RADIX = 8
SUB = NFFT // RADIX
RESIDUES = (0, 4, 1, 7, 2, 6, 3, 5)
MESH = pl.DeviceIdType.MESH


def twiddle_tables():
    n = np.arange(SUB, dtype=np.int64)[:, None]
    k2 = np.arange(CHANNELS // RADIX, dtype=np.int64)[None, :]
    scale = 1.0 / math.sqrt(NFFT)
    tables = np.zeros((4, 2 * SUB, 256), np.float64)
    for pair in range(4):
        for which in range(2):
            residue = RESIDUES[2 * pair + which]
            channel = FIRST_CH + RADIX * k2 + residue
            angle = ((n * channel) % NFFT) * (2.0 * math.pi / NFFT)
            cos, sin = np.cos(angle) * scale, np.sin(angle) * scale
            re, im = slice(which * 64, which * 64 + 64), slice(128 + which * 64, 192 + which * 64)
            if pair == 0:
                rows = slice(which * SUB, (which + 1) * SUB)
                tables[pair, rows, re] = cos
                tables[pair, rows, im] = -sin
            else:
                sign = 1.0 if which == 0 else -1.0
                tables[pair, :SUB, re] = cos
                tables[pair, SUB:, re] = -sign * sin
                tables[pair, :SUB, im] = -sin
                tables[pair, SUB:, im] = -sign * cos
    return tables.astype(jnp.bfloat16)


def al(x):
    return pl.multiple_of(x, 128)


def kernel(
    samples, fir, tables, group_row, pairs, out,
    volts, xs, wt, perm, fbuf, planes, spec, send, rows, cols, acc, stage,
    x_sem, w_sem, o_sem, own_sem, a2a_s, a2a_r, dir_s, dir_r, fwd_s, fwd_r, sib_s, sib_r,
):
    grp, tri = lax.axis_index("grp"), lax.axis_index("tri")
    gy, gz = grp // 4, lax.rem(grp, 4)
    cx, core = tri // 2, lax.rem(tri, 2)
    slots = pairs.shape[1]

    def group_at(dy, dz):
        return lax.rem(gy + dy, 4) * 4 + lax.rem(gz + dz, 4)

    def tri_at(dx):
        return lax.rem(cx + dx, 4) * 2 + core

    partners = [group_at(dy, dz) for dy in range(4) for dz in range(4) if (dy, dz) != (0, 0)]
    right, left, across = tri_at(1), tri_at(3), tri_at(2)
    sibling = cx * 2 + (1 - core)

    def frames_copy(i, count):
        src = pl.ds(al(i * (FSTEP * NFFT)), count * NFFT)
        dst = pl.ds(al(lax.rem(i, RING) * (FSTEP * NFFT)), count * NFFT)
        return pltpu.make_async_copy(samples.at[:, src], xs.at[:, dst], x_sem.at[i])

    for i in range(3):
        frames_copy(i, FSTEP).start()
    table_copy = pltpu.make_async_copy(tables, wt, w_sem)
    table_copy.start()

    barrier = pltpu.get_barrier_semaphore()
    for p in partners:
        pl.semaphore_signal(barrier, inc=1, device_id=(p, tri), device_id_type=MESH)
    for t in (right, left, sibling):
        pl.semaphore_signal(barrier, inc=1, device_id=(grp, t), device_id_type=MESH)

    number = lax.broadcasted_iota(jnp.int32, (64, CHANNELS), 1)
    for piece in range(RADIX):
        channel = lax.broadcasted_iota(jnp.int32, (64, CHANNELS), 0) * RADIX + RESIDUES[piece]
        groups = jnp.broadcast_to(group_row[...], (64, CHANNELS))
        mine = jnp.sum(jnp.where(number == channel, groups, 0), axis=1, keepdims=True)
        before = jnp.where((groups == mine) & (number < channel), 1, 0)
        rank = jnp.sum(before, axis=1, keepdims=True)
        one = jnp.where(number == mine * CH_GRP + rank, 1.0, 0.0)
        perm[pl.ds(piece * 64, 64), :] = one.astype(jnp.bfloat16)

    def a2a_copy(j, i):
        p = partners[i]
        return pltpu.make_async_remote_copy(
            src_ref=send.at[j, p], dst_ref=volts.at[j, tri, grp],
            send_sem=a2a_s.at[j], recv_sem=a2a_r.at[j],
            device_id=(p, tri), device_id_type=MESH)

    def own_copy(j):
        return pltpu.make_async_copy(send.at[j, grp], volts.at[j, tri, grp], own_sem.at[j])

    def part_copy(j, t, half, to, ssem, rsem):
        ref = volts.at[j, t] if half is None else volts.at[j, t, pl.ds(half * 8, 8)]
        return pltpu.make_async_remote_copy(
            src_ref=ref, dst_ref=ref, send_sem=ssem, recv_sem=rsem,
            device_id=(grp, to), device_id_type=MESH)

    def direct(j, way):
        return part_copy(j, tri, None, (right, left)[way], dir_s.at[way, j], dir_r.at[way, j])

    def forward(j, way):
        return part_copy(j, (left, right)[way], way, (right, left)[way], fwd_s.at[way, j], fwd_r.at[way, j])

    def share(j, which):
        return part_copy(j, (tri, left, right, across)[which], None, sibling, sib_s.at[which, j], sib_r.at[which, j])

    def stage_direct(j):
        own_copy(j).wait()
        some = volts.at[j, tri, pl.ds(0, GROUPS - 1)]
        pltpu.make_async_copy(some, some, a2a_r.at[j]).wait()
        for way in range(2):
            direct(j, way).start()
        share(j, 0).start()

    def stage_forward(j):
        for way in range(2):
            direct(j, way).wait_recv()
            forward(j, way).start()
        share(j, 1).start()
        share(j, 2).start()

    def stage_across(j):
        for way in range(2):
            forward(j, way).wait_recv()
        share(j, 3).start()

    half_root = math.sqrt(0.5)
    lane = lax.broadcasted_iota(jnp.int32, (DISH, 128), 1)

    def filter_tile(j, i):
        base = [lax.rem(j + k, RING) * (FSTEP * NFFT) for k in range(3)]
        for n1 in range(RADIX):
            off = n1 * SUB + i * 128
            coef = [fir[pl.ds(t, 1), pl.ds(al(off), 128)] for t in range(TAPS)]
            accs = [None] * FSTEP
            for fr in range(FSTEP + TAPS - 1):
                at = al(base[fr // FSTEP] + (fr % FSTEP) * NFFT + off)
                x = xs[:, pl.ds(at, 128)].astype(jnp.float32)
                for f in range(max(0, fr - TAPS + 1), min(FSTEP - 1, fr) + 1):
                    term = x * coef[fr - f]
                    accs[f] = term if accs[f] is None else accs[f] + term
                    if fr - f == TAPS - 1:
                        fbuf[n1, pl.ds(f * DISH, DISH), :] = accs[f]
        for f in range(FSTEP):
            at = pl.ds(f * DISH, DISH)
            v = [fbuf[n1, at, :] for n1 in range(RADIX)]
            a = [v[k] + v[k + 4] for k in range(4)]
            b = [v[k] - v[k + 4] for k in range(4)]
            even, odd = a[0] + a[2], a[1] + a[3]
            diff = (b[1] - b[3]) * half_root
            total = (b[1] + b[3]) * half_root
            res = (even + odd, even - odd, b[0] + diff, b[2] + total,
                   a[0] - a[2], a[1] - a[3], b[0] - diff, total - b[2])
            for k in range(RADIX):
                planes[at, pl.ds(al(k * SUB + i * 128), 128)] = res[k].astype(jnp.bfloat16)

    def transform(j):
        for p in range(4):
            got = jnp.dot(planes[:, p * 2048 : (p + 1) * 2048], wt[p], preferred_element_type=jnp.float32)
            got = got.astype(jnp.bfloat16)
            for part in range(2):
                spec[part * MROWS : (part + 1) * MROWS, p * 128 : (p + 1) * 128] = got[:, part * 128 : (part + 1) * 128]
        for two in range(2):
            sorted_ = jnp.dot(spec[...], perm[:, two * 256 : (two + 1) * 256], preferred_element_type=jnp.float32)
            for one in range(2):
                blk = sorted_[:, one * 128 : (one + 1) * 128]
                re = [blk[f * DISH : (f + 1) * DISH] for f in range(FSTEP)]
                im = [blk[MROWS + f * DISH : MROWS + (f + 1) * DISH] for f in range(FSTEP)]
                for hi in range(2):
                    if hi:
                        t = [jnp.where(lane < 64, pltpu.roll(r, 64, 1), m) for r, m in zip(re, im)]
                    else:
                        t = [jnp.where(lane < 64, r, pltpu.roll(m, 64, 1)) for r, m in zip(re, im)]
                    for bit in range(3):
                        hop = 1 << bit
                        odd = (lane >> (3 + bit)) & 1 == 1
                        new = list(t)
                        for k in range(FSTEP):
                            if not k & hop:
                                up = pltpu.roll(t[k + hop], 8 * hop, 1)
                                down = pltpu.roll(t[k], 128 - 8 * hop, 1)
                                new[k] = jnp.where(odd, up, t[k])
                                new[k + hop] = jnp.where(odd, t[k + hop], down)
                        t = new
                    for k in range(FSTEP):
                        send[j, two * 8 + one * 4 + hi * 2 + k // 4, k % 4] = t[k].astype(jnp.bfloat16)

    def correlate(k):
        for j in (2 * k, 2 * k + 1):
            for which in range(4):
                share(j, which).wait_recv()

        def row(o, carry):
            def arrange(b, c):
                for h in range(2):
                    v = volts[2 * k + h, :, b, o].reshape(BLOCK, 128)
                    rows[b, :, h * 128 : (h + 1) * 128] = v
                    vt = v.T
                    cols[b, h * 128 : (h + 1) * 128, 0:128] = vt
                    cols[b, h * 128 : h * 128 + 64, 128:256] = -vt[64:]
                    cols[b, h * 128 + 64 : (h + 1) * 128, 128:256] = vt[:64]
                return c

            lax.fori_loop(0, NBLK, arrange, 0, unroll=4)
            for s in range(slots):
                got = jnp.dot(rows[pairs[0, s]], cols[pairs[1, s]], preferred_element_type=jnp.float32)
                if k > 0:
                    got = got + acc[o, s]
                if k < CHUNKS // 2 - 1:
                    acc[o, s] = got
                else:
                    got = (got * (1.0 / (SPECTRA * FAVG))).astype(jnp.bfloat16)
                    for part in range(2):
                        stage[o, s, part] = got[:, part * 128 : (part + 1) * 128]
            if k == CHUNKS // 2 - 1:
                pltpu.make_async_copy(stage.at[o], out.at[o], o_sem.at[o]).start()
            return carry

        lax.fori_loop(0, ROWS, row, 0)

    def tiles(s, lo, hi):
        def tile(i, c):
            filter_tile(s, i)
            return c

        lax.fori_loop(lo, hi, tile, 0)

    def ship(s):
        transform(s)
        for i in range(GROUPS - 1):
            a2a_copy(s, i).start()
        own_copy(s).start()

    frames_copy(3, FSTEP).start()
    for i in range(3):
        frames_copy(i, FSTEP).wait()
    tiles(0, 0, SUB // 128)
    pl.semaphore_wait(barrier, len(partners) + 3)
    table_copy.wait()
    ship(0)

    def step(s, carry):
        @pl.when(s + 3 < CHUNKS + 1)
        def _():
            frames_copy(s + 3, FSTEP).start()

        @pl.when(s + 3 == CHUNKS + 1)
        def _():
            frames_copy(CHUNKS + 1, FSTEP - 1).start()

        @pl.when(s + 2 < CHUNKS + 1)
        def _():
            frames_copy(s + 2, FSTEP).wait()

        @pl.when(s + 2 == CHUNKS + 1)
        def _():
            frames_copy(CHUNKS + 1, FSTEP - 1).wait()

        tiles(s, 0, 5)
        stage_direct(s - 1)
        tiles(s, 5, SUB // 128)

        @pl.when(s >= 2)
        def _():
            stage_forward(s - 2)

        ship(s)

        @pl.when(s >= 3)
        def _():
            stage_across(s - 3)

        return carry

    lax.fori_loop(1, CHUNKS, step, 0)
    stage_direct(CHUNKS - 1)
    stage_forward(CHUNKS - 2)
    stage_across(CHUNKS - 3)
    correlate(0)
    stage_forward(CHUNKS - 1)
    stage_across(CHUNKS - 2)
    correlate(1)
    stage_across(CHUNKS - 1)
    correlate(2)
    correlate(3)

    def finish(j, carry):
        some = send.at[j, pl.ds(0, GROUPS - 1)]
        pltpu.make_async_copy(some, some, a2a_s.at[j]).wait()
        for way in range(2):
            direct(j, way).wait_send()
            forward(j, way).wait_send()
        for which in range(4):
            share(j, which).wait_send()
        return carry

    lax.fori_loop(0, CHUNKS, finish, 0)
    for o in range(ROWS):
        pltpu.make_async_copy(stage.at[o], out.at[o], o_sem.at[o]).wait()


def shards(samples, fir_taps, channel_group, tile_pairs):
    slots = tile_pairs.shape[1]
    tables = jnp.asarray(twiddle_tables())
    dma = pltpu.SemaphoreType.DMA
    any_spec = pl.BlockSpec(memory_space=pl.ANY)
    vmem = pl.BlockSpec(memory_space=pltpu.VMEM)
    smem = pl.BlockSpec(memory_space=pltpu.SMEM)
    return pl.pallas_call(
        kernel,
        out_shape=jax.ShapeDtypeStruct((ROWS, slots, 2, BLOCK, BLOCK), jnp.bfloat16),
        in_specs=[any_spec, vmem, any_spec, vmem, smem],
        out_specs=any_spec,
        scratch_shapes=[
            pltpu.VMEM((CHUNKS, TRI, NBLK, ROWS, DISH, 128), jnp.bfloat16),
            pltpu.VMEM((DISH, RING * FSTEP * NFFT), jnp.bfloat16),
            pltpu.VMEM(tables.shape, jnp.bfloat16),
            pltpu.VMEM((CHANNELS, CHANNELS), jnp.bfloat16),
            pltpu.VMEM((RADIX, MROWS, 128), jnp.float32),
            pltpu.VMEM((MROWS, NFFT), jnp.bfloat16),
            pltpu.VMEM((2 * MROWS, CHANNELS), jnp.bfloat16),
            pltpu.VMEM((CHUNKS, GROUPS, ROWS, DISH, 128), jnp.bfloat16),
            pltpu.VMEM((NBLK, BLOCK, 256), jnp.bfloat16),
            pltpu.VMEM((NBLK, 256, 256), jnp.bfloat16),
            pltpu.VMEM((ROWS, slots, BLOCK, 256), jnp.float32),
            pltpu.VMEM((ROWS, slots, 2, BLOCK, BLOCK), jnp.bfloat16),
            dma((CHUNKS + 2,)), dma, dma((ROWS,)), dma((CHUNKS,)), dma((CHUNKS,)), dma((CHUNKS,)),
            dma((2, CHUNKS)), dma((2, CHUNKS)), dma((2, CHUNKS)), dma((2, CHUNKS)),
            dma((4, CHUNKS)), dma((4, CHUNKS)),
        ],
        compiler_params=pltpu.CompilerParams(
            collective_id=0, has_side_effects=True, vmem_limit_bytes=58 << 20),
        name="correlator",
    )(samples, fir_taps, tables, channel_group.reshape(1, CHANNELS), tile_pairs)


def solution(mesh):
    in_specs = (P(("grp", "tri"), None), P(), P(), P(None, "tri"))
    out_specs = P("grp", "tri", None, None, None)
    return jax.shard_map(shards, mesh=mesh, in_specs=in_specs, out_specs=out_specs, check_vma=False)
```

time: 175 us -> 115 us (0.66); the launches traced: 175 us -> 113 us
  Pallas kernels: 170 us -> 107 us
    pallas_call x2 -> x1, Pallas kernels: 170 us -> 107 us  [shards(): pl.pallas_call(kernel, out_shape=jax.ShapeDtypeStruct((ROWS, slots, 2, BL...]
    unnamed x4 -> x1, local copies, waits for them, and re-layouts: 0.01 us -> 6.08 us
    gather x1 -> x0, local copies, waits for them, and re-layouts: 3.48 us -> none  [shards(): by_residue = channel_group[order]]
where the time goes in v2:
time: 115 us; the launch traced here: 113 us
  Pallas kernels  107 us (93%)
  local copies, waits for them, and re-layouts  6.08 us (5%)
    pallas_call x1, Pallas kernels, shards(): pl.pallas_call(kernel, out_shape=jax.ShapeDtypeStruct((ROWS, slots, 2, BL...  107 us
    unnamed x1, local copies, waits for them, and re-layouts  6.08 us

profile of v2, /device:TPU:1, one launch (start us, length us, event | category | flops | bytes accessed | tf_op | source)
XLA Modules:
  0.0 112.9 jit_solution(967201908090344309)
XLA Ops:
  0.0 106.8 %correlator.1 = bf16[4,17,2,128,128]{4,3,2,1,0:T(8,128)(2,1)} custom-call(bf16[16,647168]{1,0:T(8,128)(2,1)} %samples.1, f32[16,8192]{1,0:T(8,128)} %fir.1, bf16[4,2048,256]{2,1,0:T(8,128)(2,1)} %constant.2.clone.tables, s32[1,512]{1,0:T(1,128)} %bitcast.1, s32[2,17]{1,0:T(2,128)} %pairs.1), custom_call_target="tpu_custom_call" | custom-call | tf_op jit(solution)/shard_map/correlator/pallas_call | solution.py:336
  106.8 6.1 %copy.7 = bf16[4,17,2,128,128]{4,3,2,1,0:T(8,128)(2,1)} copy(bf16[4,17,2,128,128]{4,3,2,1,0:T(8,128)(2,1)} %correlator.1) | data formatting | bytes 8912896

commit v3 on v2

--- a/solution.py
+++ b/solution.py
@@ -24,6 +24,8 @@
 FSTEP = 8
 CHUNKS = SPECTRA // FSTEP
 MROWS = FSTEP * DISH
+FAR = (range(0, 8), range(8, 17))
+PIECES = ((0, 2, 4, 8), (8, 10, 13, 17))
 RING = 4
 RADIX = 8
 SUB = NFFT // RADIX
@@ -61,14 +63,15 @@
 
 
 def kernel(
-    samples, fir, tables, group_row, pairs, out,
-    volts, xs, wt, perm, fbuf, planes, spec, send, rows, cols, acc, stage,
-    x_sem, w_sem, o_sem, own_sem, a2a_s, a2a_r, dir_s, dir_r, fwd_s, fwd_r, sib_s, sib_r,
+    samples, fir, tables, group_row, pairs, own_pairs, out,
+    volts, mine4, pairs_in, near_pairs, xs, wt, perm, fbuf, planes, spec, send, rows, cols, acc, stage,
+    x_sem, w_sem, o_s, o_r, p_s, p_r, p_l, own_sem, a2a_s, a2a_r, dir_s, dir_r, fwd_s, fwd_r, sib_s, sib_r,
 ):
     grp, tri = lax.axis_index("grp"), lax.axis_index("tri")
     gy, gz = grp // 4, lax.rem(grp, 4)
     cx, core = tri // 2, lax.rem(tri, 2)
-    slots = pairs.shape[1]
+    slots = own_pairs.shape[1]
+    last = CHUNKS // 2 - 1
 
     def group_at(dy, dz):
         return lax.rem(gy + dy, 4) * 4 + lax.rem(gz + dz, 4)
@@ -109,46 +112,68 @@
     def a2a_copy(j, i):
         p = partners[i]
         return pltpu.make_async_remote_copy(
-            src_ref=send.at[j, p], dst_ref=volts.at[j, tri, grp],
+            src_ref=send.at[j, p], dst_ref=mine4.at[j, :, grp],
             send_sem=a2a_s.at[j], recv_sem=a2a_r.at[j],
             device_id=(p, tri), device_id_type=MESH)
 
     def own_copy(j):
-        return pltpu.make_async_copy(send.at[j, grp], volts.at[j, tri, grp], own_sem.at[j])
-
-    def part_copy(j, t, half, to, ssem, rsem):
-        ref = volts.at[j, t] if half is None else volts.at[j, t, pl.ds(half * 8, 8)]
+        return pltpu.make_async_copy(send.at[j, grp], mine4.at[j, :, grp], own_sem.at[0, j])
+
+    def keep_copy(j):
+        return pltpu.make_async_copy(mine4.at[j, pl.ds(1, 3)], volts.at[j, tri], own_sem.at[1, j])
+
+    def remote(src, dst, to, ssem, rsem):
         return pltpu.make_async_remote_copy(
-            src_ref=ref, dst_ref=ref, send_sem=ssem, recv_sem=rsem,
+            src_ref=src, dst_ref=dst, send_sem=ssem, recv_sem=rsem,
             device_id=(grp, to), device_id_type=MESH)
 
-    def direct(j, way):
-        return part_copy(j, tri, None, (right, left)[way], dir_s.at[way, j], dir_r.at[way, j])
-
-    def forward(j, way):
-        return part_copy(j, (left, right)[way], way, (right, left)[way], fwd_s.at[way, j], fwd_r.at[way, j])
+    def direct(j, part):
+        if part == 0:
+            src, dst, way = mine4.at[j, pl.ds(2, 2)], volts.at[j, tri, pl.ds(0, 2)], 0
+        elif part == 1:
+            src, dst, way = mine4.at[j, 0], volts.at[j, tri, 2], 0
+        else:
+            src, dst, way = mine4.at[j, pl.ds(0, 3)], volts.at[j, tri], 1
+        return remote(src, dst, (right, left)[way], dir_s.at[part, j], dir_r.at[part, j])
+
+    def forward(j, way, whole):
+        t = (left, right)[way]
+        if whole:
+            src, dst = volts.at[j, t, 1], volts.at[j, t, 2 * way]
+        else:
+            half = pl.ds(8 * way, 8)
+            src, dst = volts.at[j, t, 2 - 2 * way, half], volts.at[j, t, 1, half]
+        return remote(src, dst, (right, left)[way], fwd_s.at[way, whole, j], fwd_r.at[way, whole, j])
 
     def share(j, which):
-        return part_copy(j, (tri, left, right, across)[which], None, sibling, sib_s.at[which, j], sib_r.at[which, j])
+        t = (tri, left, right, across)[which]
+        src = mine4.at[j, pl.ds(1, 3)] if which == 0 else volts.at[j, t]
+        return remote(src, volts.at[j, t], sibling, sib_s.at[which, j], sib_r.at[which, j])
 
     def stage_direct(j):
         own_copy(j).wait()
-        some = volts.at[j, tri, pl.ds(0, GROUPS - 1)]
+        some = mine4.at[j, :, pl.ds(0, GROUPS - 1)]
         pltpu.make_async_copy(some, some, a2a_r.at[j]).wait()
-        for way in range(2):
-            direct(j, way).start()
+        for part in (2, 0, 1):
+            direct(j, part).start()
         share(j, 0).start()
+        keep_copy(j).start()
 
     def stage_forward(j):
-        for way in range(2):
-            direct(j, way).wait_recv()
-            forward(j, way).start()
+        direct(j, 2).wait_recv()
+        for whole in (1, 0):
+            forward(j, 1, whole).start()
+        direct(j, 0).wait_recv()
+        direct(j, 1).wait_recv()
+        for whole in (1, 0):
+            forward(j, 0, whole).start()
         share(j, 1).start()
         share(j, 2).start()
 
     def stage_across(j):
         for way in range(2):
-            forward(j, way).wait_recv()
+            for whole in range(2):
+                forward(j, way, whole).wait_recv()
         share(j, 3).start()
 
     half_root = math.sqrt(0.5)
@@ -210,40 +235,76 @@
                                 new[k + hop] = jnp.where(odd, t[k + hop], down)
                         t = new
                     for k in range(FSTEP):
-                        send[j, two * 8 + one * 4 + hi * 2 + k // 4, k % 4] = t[k].astype(jnp.bfloat16)
-
-    def correlate(k):
+                        send[j, two * 8 + one * 4 + hi * 2 + k // 4, lax.rem(k % 4 + 6 - cx, 4)] = t[k].astype(jnp.bfloat16)
+
+    def arrived(k):
         for j in (2 * k, 2 * k + 1):
+            keep_copy(j).wait()
             for which in range(4):
                 share(j, which).wait_recv()
 
-        def row(o, carry):
-            def arrange(b, c):
-                for h in range(2):
-                    v = volts[2 * k + h, :, b, o].reshape(BLOCK, 128)
-                    rows[b, :, h * 128 : (h + 1) * 128] = v
-                    vt = v.T
-                    cols[b, h * 128 : (h + 1) * 128, 0:128] = vt
-                    cols[b, h * 128 : h * 128 + 64, 128:256] = -vt[64:]
-                    cols[b, h * 128 + 64 : (h + 1) * 128, 128:256] = vt[:64]
-                return c
-
-            lax.fori_loop(0, NBLK, arrange, 0, unroll=4)
+    def arrange(k, r, slot):
+        def block(b, c):
+            for h in range(2):
+                v = volts[2 * k + h, :, r, b].reshape(BLOCK, 128)
+                rows[slot, b, :, h * 128 : (h + 1) * 128] = v
+                vt = v.T
+                cols[slot, b, h * 128 : (h + 1) * 128, 0:128] = vt
+                cols[slot, b, h * 128 : h * 128 + 64, 128:256] = -vt[64:]
+                cols[slot, b, h * 128 + 64 : (h + 1) * 128, 128:256] = vt[:64]
+            return c
+
+        lax.fori_loop(0, NBLK, block, 0, unroll=4)
+
+    def product(slot, ref, s):
+        return jnp.dot(rows[slot, ref[0, s]], cols[slot, ref[1, s]], preferred_element_type=jnp.float32)
+
+    def correlate(k):
+        arrived(k)
+
+        def add(r, slot, ref, s):
+            got = product(slot, ref, s)
+            acc[r, s] = got if k == 0 else got + acc[r, s]
+
+        for r, slot in ((0, 0), (2, 1), (1, 0)):
+            arrange(k, r, slot)
             for s in range(slots):
-                got = jnp.dot(rows[pairs[0, s]], cols[pairs[1, s]], preferred_element_type=jnp.float32)
-                if k > 0:
-                    got = got + acc[o, s]
-                if k < CHUNKS // 2 - 1:
-                    acc[o, s] = got
-                else:
-                    got = (got * (1.0 / (SPECTRA * FAVG))).astype(jnp.bfloat16)
+                add(r, slot, own_pairs, s)
+            if r != 1:
+                for s in FAR[slot]:
+                    add(3, slot, near_pairs.at[slot], s)
+
+    def result(r, slot, ref, s):
+        got = (product(slot, ref, s) + acc[r, s]) * (1.0 / (SPECTRA * FAVG))
+        return got.astype(jnp.bfloat16)
+
+    def deliver(slot, piece):
+        lo, hi = PIECES[slot][piece], PIECES[slot][piece + 1]
+        part = pl.ds(lo, hi - lo)
+        return remote(stage.at[part], out.at[lax.rem(cx + 3 + 2 * slot, 4), part], (right, left)[slot],
+                      o_s.at[slot, piece], o_r.at[slot, piece])
+
+    def final():
+        arrived(last)
+        for slot in range(2):
+            arrange(last, 2 * slot, slot)
+            for piece in range(len(PIECES[slot]) - 1):
+                for s in range(PIECES[slot][piece], PIECES[slot][piece + 1]):
+                    got = result(3, slot, near_pairs.at[slot], s)
                     for part in range(2):
-                        stage[o, s, part] = got[:, part * 128 : (part + 1) * 128]
-            if k == CHUNKS // 2 - 1:
-                pltpu.make_async_copy(stage.at[o], out.at[o], o_sem.at[o]).start()
-            return carry
-
-        lax.fori_loop(0, ROWS, row, 0)
+                        stage[s, part] = got[:, part * 128 : (part + 1) * 128]
+                deliver(slot, piece).start()
+        for r, slot in ((0, 0), (2, 1), (1, 0)):
+            if r == 1:
+                arrange(last, r, slot)
+            row = lax.rem(cx + 3 + r, 4)
+            for s in range(slots):
+                got = result(r, slot, own_pairs, s)
+                for part in range(2):
+                    out[row, s, part] = got[:, part * 128 : (part + 1) * 128]
+
+    def pairs_copy(way):
+        return remote(pairs, pairs_in.at[way], (left, right)[way], p_s.at[way], p_r.at[way])
 
     def tiles(s, lo, hi):
         def tile(i, c):
@@ -264,6 +325,8 @@
     tiles(0, 0, SUB // 128)
     pl.semaphore_wait(barrier, len(partners) + 3)
     table_copy.wait()
+    for way in range(2):
+        pairs_copy(way).start()
     ship(0)
 
     def step(s, carry):
@@ -283,51 +346,59 @@
         def _():
             frames_copy(CHUNKS + 1, FSTEP - 1).wait()
 
-        tiles(s, 0, 5)
+        tiles(s, 0, SUB // 128)
         stage_direct(s - 1)
-        tiles(s, 5, SUB // 128)
 
         @pl.when(s >= 2)
         def _():
             stage_forward(s - 2)
 
+        @pl.when(s >= 3)
+        def _():
+            stage_across(s - 3)
+
         ship(s)
-
-        @pl.when(s >= 3)
-        def _():
-            stage_across(s - 3)
-
         return carry
 
     lax.fori_loop(1, CHUNKS, step, 0)
-    stage_direct(CHUNKS - 1)
+    for way in range(2):
+        pairs_copy(way).wait()
+        pltpu.make_async_copy(pairs_in.at[way], near_pairs.at[way], p_l.at[way]).start()
+    for way in range(2):
+        pltpu.make_async_copy(pairs_in.at[way], near_pairs.at[way], p_l.at[way]).wait()
+    correlate(0)
     stage_forward(CHUNKS - 2)
     stage_across(CHUNKS - 3)
-    correlate(0)
+    stage_direct(CHUNKS - 1)
+    correlate(1)
     stage_forward(CHUNKS - 1)
     stage_across(CHUNKS - 2)
-    correlate(1)
+    correlate(2)
     stage_across(CHUNKS - 1)
-    correlate(2)
-    correlate(3)
+    final()
 
     def finish(j, carry):
         some = send.at[j, pl.ds(0, GROUPS - 1)]
         pltpu.make_async_copy(some, some, a2a_s.at[j]).wait()
+        for part in range(3):
+            direct(j, part).wait_send()
         for way in range(2):
-            direct(j, way).wait_send()
-            forward(j, way).wait_send()
+            for whole in range(2):
+                forward(j, way, whole).wait_send()
         for which in range(4):
             share(j, which).wait_send()
         return carry
 
     lax.fori_loop(0, CHUNKS, finish, 0)
-    for o in range(ROWS):
-        pltpu.make_async_copy(stage.at[o], out.at[o], o_sem.at[o]).wait()
+    for slot in range(2):
+        for piece in range(len(PIECES[slot]) - 1):
+            deliver(slot, piece).wait_send()
+            deliver(slot, piece).wait_recv()
 
 
 def shards(samples, fir_taps, channel_group, tile_pairs):
     slots = tile_pairs.shape[1]
+    pieces = len(PIECES[0]) - 1
     tables = jnp.asarray(twiddle_tables())
     dma = pltpu.SemaphoreType.DMA
     any_spec = pl.BlockSpec(memory_space=pl.ANY)
@@ -335,11 +406,14 @@
     smem = pl.BlockSpec(memory_space=pltpu.SMEM)
     return pl.pallas_call(
         kernel,
-        out_shape=jax.ShapeDtypeStruct((ROWS, slots, 2, BLOCK, BLOCK), jnp.bfloat16),
-        in_specs=[any_spec, vmem, any_spec, vmem, smem],
-        out_specs=any_spec,
+        out_shape=pltpu.VMEM((ROWS, slots, 2, BLOCK, BLOCK), jnp.bfloat16),
+        in_specs=[any_spec, vmem, any_spec, vmem, any_spec, smem],
+        out_specs=vmem,
         scratch_shapes=[
-            pltpu.VMEM((CHUNKS, TRI, NBLK, ROWS, DISH, 128), jnp.bfloat16),
+            pltpu.VMEM((CHUNKS, TRI, 3, NBLK, DISH, 128), jnp.bfloat16),
+            pltpu.VMEM((CHUNKS, ROWS, NBLK, DISH, 128), jnp.bfloat16),
+            pltpu.VMEM((2, 2, slots), jnp.int32),
+            pltpu.SMEM((2, 2, slots), jnp.int32),
             pltpu.VMEM((DISH, RING * FSTEP * NFFT), jnp.bfloat16),
             pltpu.VMEM(tables.shape, jnp.bfloat16),
             pltpu.VMEM((CHANNELS, CHANNELS), jnp.bfloat16),
@@ -347,18 +421,19 @@
             pltpu.VMEM((MROWS, NFFT), jnp.bfloat16),
             pltpu.VMEM((2 * MROWS, CHANNELS), jnp.bfloat16),
             pltpu.VMEM((CHUNKS, GROUPS, ROWS, DISH, 128), jnp.bfloat16),
-            pltpu.VMEM((NBLK, BLOCK, 256), jnp.bfloat16),
-            pltpu.VMEM((NBLK, 256, 256), jnp.bfloat16),
-            pltpu.VMEM((ROWS, slots, BLOCK, 256), jnp.float32),
-            pltpu.VMEM((ROWS, slots, 2, BLOCK, BLOCK), jnp.bfloat16),
-            dma((CHUNKS + 2,)), dma, dma((ROWS,)), dma((CHUNKS,)), dma((CHUNKS,)), dma((CHUNKS,)),
-            dma((2, CHUNKS)), dma((2, CHUNKS)), dma((2, CHUNKS)), dma((2, CHUNKS)),
+            pltpu.VMEM((2, NBLK, BLOCK, 256), jnp.bfloat16),
+            pltpu.VMEM((2, NBLK, 256, 256), jnp.bfloat16),
+            pltpu.VMEM((4, slots, BLOCK, 256), jnp.float32),
+            pltpu.VMEM((slots, 2, BLOCK, BLOCK), jnp.bfloat16),
+            dma((CHUNKS + 2,)), dma, dma((2, pieces)), dma((2, pieces)), dma((2,)), dma((2,)), dma((2,)),
+            dma((2, CHUNKS)), dma((CHUNKS,)), dma((CHUNKS,)),
+            dma((3, CHUNKS)), dma((3, CHUNKS)), dma((2, 2, CHUNKS)), dma((2, 2, CHUNKS)),
             dma((4, CHUNKS)), dma((4, CHUNKS)),
         ],
         compiler_params=pltpu.CompilerParams(
-            collective_id=0, has_side_effects=True, vmem_limit_bytes=58 << 20),
+            collective_id=0, has_side_effects=True, vmem_limit_bytes=56 << 20),
         name="correlator",
-    )(samples, fir_taps, tables, channel_group.reshape(1, CHANNELS), tile_pairs)
+    )(samples, fir_taps, tables, channel_group.reshape(1, CHANNELS), tile_pairs, tile_pairs)
 
 
 def solution(mesh):

time: 115 us -> 104 us (0.904); the launches traced: 113 us -> 104 us
  Pallas kernels: 107 us -> 102 us
  local copies, waits for them, and re-layouts: 6.08 us -> 2.1 us
    pallas_call x1, Pallas kernels: 107 us -> 102 us  [shards(): pl.pallas_call(kernel, out_shape=pltpu.VMEM((ROWS, slots, 2, BLOCK, BLOCK...]
    unnamed x1, local copies, waits for them, and re-layouts: 6.08 us -> 2.1 us
where the time goes in v3:
time: 104 us
  Pallas kernels  102 us (98%)
  local copies, waits for them, and re-layouts  2.1 us (2%)
    pallas_call x1, Pallas kernels, shards(): pl.pallas_call(kernel, out_shape=pltpu.VMEM((ROWS, slots, 2, BLOCK, BLOCK...  102 us
    unnamed x1, local copies, waits for them, and re-layouts  2.1 us

profile of v3, /device:TPU:1, one launch (start us, length us, event | category | flops | bytes accessed | tf_op | source)
XLA Modules:
  0.0 103.9 jit_solution(9261168882390590209)
XLA Ops:
  0.0 101.8 %correlator.1 = bf16[4,17,2,128,128]{4,3,2,1,0:T(8,128)(2,1)S(1)} custom-call(bf16[16,647168]{1,0:T(8,128)(2,1)} %samples.1, f32[16,8192]{1,0:T(8,128)} %fir.1, bf16[4,2048,256]{2,1,0:T(8,128)(2,1)} %constant.2.clone.tables, s32[1,512]{1,0:T(1,128)} %bitcast.1, s32[2,17]{1,0:T(2,128)} %own_pairs.1, s32[2,17]{1,0:T(2,128)} %own_pairs.1), custom_call_target="tpu_custom_call" | custom-call | tf_op jit(solution)/shard_map/correlator/pallas_call | solution.py:407
  101.8 2.1 %copy.7 = bf16[4,17,2,128,128]{4,3,2,1,0:T(8,128)(2,1)} copy(bf16[4,17,2,128,128]{4,3,2,1,0:T(8,128)(2,1)S(1)} %correlator.1) | data formatting | bytes 8912896

commit v4 on v3

--- a/solution.py
+++ b/solution.py
@@ -24,8 +24,8 @@
 FSTEP = 8
 CHUNKS = SPECTRA // FSTEP
 MROWS = FSTEP * DISH
-FAR = (range(0, 8), range(8, 17))
-PIECES = ((0, 2, 4, 8), (8, 10, 13, 17))
+FAR = (range(0, 9), range(9, 17))
+PIECES = ((0, 2, 5, 9), (9, 11, 13, 17))
 RING = 4
 RADIX = 8
 SUB = NFFT // RADIX
@@ -63,8 +63,8 @@
 
 
 def kernel(
-    samples, fir, tables, group_row, pairs, own_pairs, out,
-    volts, mine4, pairs_in, near_pairs, xs, wt, perm, fbuf, planes, spec, send, rows, cols, acc, stage,
+    samples, taps, tables, group_row, pairs, own_pairs, out,
+    volts, mine4, pairs_in, near_pairs, xs, fir, wt, perm, fbuf, planes, spec, send, rows, cols, acc, stage,
     x_sem, w_sem, o_s, o_r, p_s, p_r, p_l, own_sem, a2a_s, a2a_r, dir_s, dir_r, fwd_s, fwd_r, sib_s, sib_r,
 ):
     grp, tri = lax.axis_index("grp"), lax.axis_index("tri")
@@ -88,10 +88,11 @@
         dst = pl.ds(al(lax.rem(i, RING) * (FSTEP * NFFT)), count * NFFT)
         return pltpu.make_async_copy(samples.at[:, src], xs.at[:, dst], x_sem.at[i])
 
+    table_copy = pltpu.make_async_copy(tables, wt, w_sem.at[0])
+    taps_copy = pltpu.make_async_copy(taps, fir, w_sem.at[1])
+    taps_copy.start()
     for i in range(3):
         frames_copy(i, FSTEP).start()
-    table_copy = pltpu.make_async_copy(tables, wt, w_sem)
-    table_copy.start()
 
     barrier = pltpu.get_barrier_semaphore()
     for p in partners:
@@ -216,26 +217,15 @@
             sorted_ = jnp.dot(spec[...], perm[:, two * 256 : (two + 1) * 256], preferred_element_type=jnp.float32)
             for one in range(2):
                 blk = sorted_[:, one * 128 : (one + 1) * 128]
-                re = [blk[f * DISH : (f + 1) * DISH] for f in range(FSTEP)]
-                im = [blk[MROWS + f * DISH : MROWS + (f + 1) * DISH] for f in range(FSTEP)]
-                for hi in range(2):
-                    if hi:
-                        t = [jnp.where(lane < 64, pltpu.roll(r, 64, 1), m) for r, m in zip(re, im)]
-                    else:
-                        t = [jnp.where(lane < 64, r, pltpu.roll(m, 64, 1)) for r, m in zip(re, im)]
-                    for bit in range(3):
-                        hop = 1 << bit
-                        odd = (lane >> (3 + bit)) & 1 == 1
-                        new = list(t)
-                        for k in range(FSTEP):
-                            if not k & hop:
-                                up = pltpu.roll(t[k + hop], 8 * hop, 1)
-                                down = pltpu.roll(t[k], 128 - 8 * hop, 1)
-                                new[k] = jnp.where(odd, up, t[k])
-                                new[k + hop] = jnp.where(odd, t[k + hop], down)
-                        t = new
-                    for k in range(FSTEP):
-                        send[j, two * 8 + one * 4 + hi * 2 + k // 4, lax.rem(k % 4 + 6 - cx, 4)] = t[k].astype(jnp.bfloat16)
+                t = []
+                for k in range(2 * FSTEP):
+                    v = blk[k * DISH : (k + 1) * DISH]
+                    t.append(pltpu.roll(v, 8 * k, 1) if k else v)
+                for bit in range(4):
+                    odd = (lane >> (3 + bit)) & 1 == 1
+                    t = [jnp.where(odd, t[(k + (1 << bit)) % 16], t[k]) for k in range(16)]
+                for go in range(16):
+                    send[j, two * 8 + one * 4 + go // 4, lax.rem(go % 4 + 6 - cx, 4)] = t[-go % 16].astype(jnp.bfloat16)
 
     def arrived(k):
         for j in (2 * k, 2 * k + 1):
@@ -244,14 +234,18 @@
                 share(j, which).wait_recv()
 
     def arrange(k, r, slot):
+        go = lax.rem(grp, 4) * 4 + lax.rem(cx + 3 + r, 4)
+        place = lax.rem((lax.broadcasted_iota(jnp.int32, (BLOCK, BLOCK), 0) >> 3) - go + 16, 16)
+        sign = jnp.where(place < FSTEP, -1.0, 1.0).astype(jnp.bfloat16)
+
         def block(b, c):
             for h in range(2):
                 v = volts[2 * k + h, :, r, b].reshape(BLOCK, 128)
                 rows[slot, b, :, h * 128 : (h + 1) * 128] = v
                 vt = v.T
                 cols[slot, b, h * 128 : (h + 1) * 128, 0:128] = vt
-                cols[slot, b, h * 128 : h * 128 + 64, 128:256] = -vt[64:]
-                cols[slot, b, h * 128 + 64 : (h + 1) * 128, 128:256] = vt[:64]
+                swapped = jnp.concatenate([vt[64:], vt[:64]], axis=0)
+                cols[slot, b, h * 128 : (h + 1) * 128, 128:256] = swapped * sign
             return c
 
         lax.fori_loop(0, NBLK, block, 0, unroll=4)
@@ -306,12 +300,12 @@
     def pairs_copy(way):
         return remote(pairs, pairs_in.at[way], (left, right)[way], p_s.at[way], p_r.at[way])
 
-    def tiles(s, lo, hi):
+    def tiles(s, send_previous):
         def tile(i, c):
             filter_tile(s, i)
             return c
 
-        lax.fori_loop(lo, hi, tile, 0)
+        lax.fori_loop(0, SUB // 128, tile, 0)
 
     def ship(s):
         transform(s)
@@ -319,10 +313,12 @@
             a2a_copy(s, i).start()
         own_copy(s).start()
 
-    frames_copy(3, FSTEP).start()
+    taps_copy.wait()
     for i in range(3):
         frames_copy(i, FSTEP).wait()
-    tiles(0, 0, SUB // 128)
+    table_copy.start()
+    frames_copy(3, FSTEP).start()
+    tiles(0, False)
     pl.semaphore_wait(barrier, len(partners) + 3)
     table_copy.wait()
     for way in range(2):
@@ -346,9 +342,11 @@
         def _():
             frames_copy(CHUNKS + 1, FSTEP - 1).wait()
 
-        tiles(s, 0, SUB // 128)
+        tiles(s, True)
         stage_direct(s - 1)
 
+        ship(s)
+
         @pl.when(s >= 2)
         def _():
             stage_forward(s - 2)
@@ -357,7 +355,6 @@
         def _():
             stage_across(s - 3)
 
-        ship(s)
         return carry
 
     lax.fori_loop(1, CHUNKS, step, 0)
@@ -407,7 +404,7 @@
     return pl.pallas_call(
         kernel,
         out_shape=pltpu.VMEM((ROWS, slots, 2, BLOCK, BLOCK), jnp.bfloat16),
-        in_specs=[any_spec, vmem, any_spec, vmem, any_spec, smem],
+        in_specs=[any_spec, any_spec, any_spec, vmem, any_spec, smem],
         out_specs=vmem,
         scratch_shapes=[
             pltpu.VMEM((CHUNKS, TRI, 3, NBLK, DISH, 128), jnp.bfloat16),
@@ -415,6 +412,7 @@
             pltpu.VMEM((2, 2, slots), jnp.int32),
             pltpu.SMEM((2, 2, slots), jnp.int32),
             pltpu.VMEM((DISH, RING * FSTEP * NFFT), jnp.bfloat16),
+            pltpu.VMEM(fir_taps.shape, jnp.float32),
             pltpu.VMEM(tables.shape, jnp.bfloat16),
             pltpu.VMEM((CHANNELS, CHANNELS), jnp.bfloat16),
             pltpu.VMEM((RADIX, MROWS, 128), jnp.float32),
@@ -425,7 +423,7 @@
             pltpu.VMEM((2, NBLK, 256, 256), jnp.bfloat16),
             pltpu.VMEM((4, slots, BLOCK, 256), jnp.float32),
             pltpu.VMEM((slots, 2, BLOCK, BLOCK), jnp.bfloat16),
-            dma((CHUNKS + 2,)), dma, dma((2, pieces)), dma((2, pieces)), dma((2,)), dma((2,)), dma((2,)),
+            dma((CHUNKS + 2,)), dma((2,)), dma((2, pieces)), dma((2, pieces)), dma((2,)), dma((2,)), dma((2,)),
             dma((2, CHUNKS)), dma((CHUNKS,)), dma((CHUNKS,)),
             dma((3, CHUNKS)), dma((3, CHUNKS)), dma((2, 2, CHUNKS)), dma((2, 2, CHUNKS)),
             dma((4, CHUNKS)), dma((4, CHUNKS)),

time: 104 us -> 103 us (level)
  Pallas kernels: 102 us -> 100 us
    pallas_call x1, Pallas kernels: 102 us -> 100 us  [shards(): pl.pallas_call(kernel, out_shape=pltpu.VMEM((ROWS, slots, 2, BLOCK, BLOCK...]
where the time goes in v4:
time: 103 us; the launch traced here: 102 us
  Pallas kernels  100 us (97%)
  local copies, waits for them, and re-layouts  2.1 us (2%)
    pallas_call x1, Pallas kernels, shards(): pl.pallas_call(kernel, out_shape=pltpu.VMEM((ROWS, slots, 2, BLOCK, BLOCK...  100 us
    unnamed x1, local copies, waits for them, and re-layouts  2.1 us

profile of v4, /device:TPU:1, one launch (start us, length us, event | category | flops | bytes accessed | tf_op | source)
XLA Modules:
  0.0 102.4 jit_solution(4421447457386011970)
XLA Ops:
  0.0 100.3 %correlator.1 = bf16[4,17,2,128,128]{4,3,2,1,0:T(8,128)(2,1)S(1)} custom-call(bf16[16,647168]{1,0:T(8,128)(2,1)} %samples.1, f32[16,8192]{1,0:T(8,128)} %taps.1, bf16[4,2048,256]{2,1,0:T(8,128)(2,1)} %constant.2.clone.tables, s32[1,512]{1,0:T(1,128)} %bitcast.1, s32[2,17]{1,0:T(2,128)} %own_pairs.1, s32[2,17]{1,0:T(2,128)} %own_pairs.1), custom_call_target="tpu_custom_call" | custom-call | tf_op jit(solution)/shard_map/correlator/pallas_call | solution.py:404
  100.3 2.1 %copy.7 = bf16[4,17,2,128,128]{4,3,2,1,0:T(8,128)(2,1)} copy(bf16[4,17,2,128,128]{4,3,2,1,0:T(8,128)(2,1)S(1)} %correlator.1) | data formatting | bytes 8912896

commit v5 on v4

--- a/solution.py
+++ b/solution.py
@@ -113,15 +113,15 @@
     def a2a_copy(j, i):
         p = partners[i]
         return pltpu.make_async_remote_copy(
-            src_ref=send.at[j, p], dst_ref=mine4.at[j, :, grp],
+            src_ref=send.at[j, p], dst_ref=mine4.at[j, grp],
             send_sem=a2a_s.at[j], recv_sem=a2a_r.at[j],
             device_id=(p, tri), device_id_type=MESH)
 
     def own_copy(j):
-        return pltpu.make_async_copy(send.at[j, grp], mine4.at[j, :, grp], own_sem.at[0, j])
+        return pltpu.make_async_copy(send.at[j, grp], mine4.at[j, grp], own_sem.at[0, j])
 
     def keep_copy(j):
-        return pltpu.make_async_copy(mine4.at[j, pl.ds(1, 3)], volts.at[j, tri], own_sem.at[1, j])
+        return pltpu.make_async_copy(mine4.at[j, :, pl.ds(1, 3)], volts.at[j, tri], own_sem.at[1, j])
 
     def remote(src, dst, to, ssem, rsem):
         return pltpu.make_async_remote_copy(
@@ -130,30 +130,30 @@
 
     def direct(j, part):
         if part == 0:
-            src, dst, way = mine4.at[j, pl.ds(2, 2)], volts.at[j, tri, pl.ds(0, 2)], 0
+            src, dst, way = mine4.at[j, :, pl.ds(2, 2)], volts.at[j, tri, :, pl.ds(0, 2)], 0
         elif part == 1:
-            src, dst, way = mine4.at[j, 0], volts.at[j, tri, 2], 0
+            src, dst, way = mine4.at[j, :, 0], volts.at[j, tri, :, 2], 0
         else:
-            src, dst, way = mine4.at[j, pl.ds(0, 3)], volts.at[j, tri], 1
+            src, dst, way = mine4.at[j, :, pl.ds(0, 3)], volts.at[j, tri], 1
         return remote(src, dst, (right, left)[way], dir_s.at[part, j], dir_r.at[part, j])
 
     def forward(j, way, whole):
         t = (left, right)[way]
         if whole:
-            src, dst = volts.at[j, t, 1], volts.at[j, t, 2 * way]
+            src, dst = volts.at[j, t, :, 1], volts.at[j, t, :, 2 * way]
         else:
             half = pl.ds(8 * way, 8)
-            src, dst = volts.at[j, t, 2 - 2 * way, half], volts.at[j, t, 1, half]
+            src, dst = volts.at[j, t, half, 2 - 2 * way], volts.at[j, t, half, 1]
         return remote(src, dst, (right, left)[way], fwd_s.at[way, whole, j], fwd_r.at[way, whole, j])
 
     def share(j, which):
         t = (tri, left, right, across)[which]
-        src = mine4.at[j, pl.ds(1, 3)] if which == 0 else volts.at[j, t]
+        src = mine4.at[j, :, pl.ds(1, 3)] if which == 0 else volts.at[j, t]
         return remote(src, volts.at[j, t], sibling, sib_s.at[which, j], sib_r.at[which, j])
 
     def stage_direct(j):
         own_copy(j).wait()
-        some = mine4.at[j, :, pl.ds(0, GROUPS - 1)]
+        some = mine4.at[j, pl.ds(0, GROUPS - 1)]
         pltpu.make_async_copy(some, some, a2a_r.at[j]).wait()
         for part in (2, 0, 1):
             direct(j, part).start()
@@ -240,7 +240,7 @@
 
         def block(b, c):
             for h in range(2):
-                v = volts[2 * k + h, :, r, b].reshape(BLOCK, 128)
+                v = volts[2 * k + h, :, b, r].reshape(BLOCK, 128)
                 rows[slot, b, :, h * 128 : (h + 1) * 128] = v
                 vt = v.T
                 cols[slot, b, h * 128 : (h + 1) * 128, 0:128] = vt
@@ -407,8 +407,8 @@
         in_specs=[any_spec, any_spec, any_spec, vmem, any_spec, smem],
         out_specs=vmem,
         scratch_shapes=[
-            pltpu.VMEM((CHUNKS, TRI, 3, NBLK, DISH, 128), jnp.bfloat16),
-            pltpu.VMEM((CHUNKS, ROWS, NBLK, DISH, 128), jnp.bfloat16),
+            pltpu.VMEM((CHUNKS, TRI, NBLK, 3, DISH, 128), jnp.bfloat16),
+            pltpu.VMEM((CHUNKS, NBLK, ROWS, DISH, 128), jnp.bfloat16),
             pltpu.VMEM((2, 2, slots), jnp.int32),
             pltpu.SMEM((2, 2, slots), jnp.int32),
             pltpu.VMEM((DISH, RING * FSTEP * NFFT), jnp.bfloat16),

time: 103 us -> 102 us (level)
  no operation moved by 1% of the time
where the time goes in v5:
time: 102 us; the launch traced here: 101 us
  Pallas kernels  99.4 us (97%)
  local copies, waits for them, and re-layouts  2.1 us (2%)
    pallas_call x1, Pallas kernels, shards(): pl.pallas_call(kernel, out_shape=pltpu.VMEM((ROWS, slots, 2, BLOCK, BLOCK...  99.4 us
    unnamed x1, local copies, waits for them, and re-layouts  2.1 us

profile of v5, /device:TPU:1, one launch (start us, length us, event | category | flops | bytes accessed | tf_op | source)
XLA Modules:
  0.0 101.5 jit_solution(2887461331574852760)
XLA Ops:
  0.0 99.4 %correlator.1 = bf16[4,17,2,128,128]{4,3,2,1,0:T(8,128)(2,1)S(1)} custom-call(bf16[16,647168]{1,0:T(8,128)(2,1)} %samples.1, f32[16,8192]{1,0:T(8,128)} %taps.1, bf16[4,2048,256]{2,1,0:T(8,128)(2,1)} %constant.2.clone.tables, s32[1,512]{1,0:T(1,128)} %bitcast.1, s32[2,17]{1,0:T(2,128)} %own_pairs.1, s32[2,17]{1,0:T(2,128)} %own_pairs.1), custom_call_target="tpu_custom_call" | custom-call | tf_op jit(solution)/shard_map/correlator/pallas_call | solution.py:404
  99.4 2.1 %copy.7 = bf16[4,17,2,128,128]{4,3,2,1,0:T(8,128)(2,1)} copy(bf16[4,17,2,128,128]{4,3,2,1,0:T(8,128)(2,1)S(1)} %correlator.1) | data formatting | bytes 8912896
